TPU v7x, 32 devices: a whole 2x2x4 slice. The times are simulated.
32 devices in a mesh: parts: 2 (over y), ship: 4 (over x, core), panel: 4 (over z).
Axes of the slice: x: 2, y: 2, z: 4, core: 2. Of those that a mesh axis runs over, the one named last changes fastest.
Arguments:
- right_side: float32 [8, 2, 32, 1024], P(('parts', 'ship'), None, None, 'panel'), parts along dimension 0, may hold values from -6 to 6
- current: bfloat16 [8, 2, 32, 1024], P(('parts', 'ship'), None, None, 'panel'), parts along dimension 0, may hold values from -6 to 6
- near_values: bfloat16 [8, 8, 6, 2, 128, 128], P(('parts', 'ship'), 'panel'), parts along dimension 0, may hold values from -0.15625 to 0.15625
- near_columns: int32 [8, 8, 6], P(('parts', 'ship'), 'panel'), parts along dimension 0, may hold values from 0 to 7, as said below
- block_inverse: bfloat16 [8, 8, 2, 128, 128], P(('parts', 'ship'), 'panel'), parts along dimension 0, may hold values from -1 to 2
- coupling_right: bfloat16 [8, 4, 2, 64, 1024], P('parts', 'ship', None, None, 'panel'), parts along dimension 0, may hold values from -0.125 to 0.125
- coupling_left: bfloat16 [8, 4, 2, 64, 1024], P(('parts', 'ship'), None, None, None, 'panel'), parts along dimension 0, may hold values from -0.26171875 to 0.26171875
- pair_rank: int32 [4, 4], replicated, may hold values from 32 to 64
- plan: int32 [3, 4], replicated, may hold values from 0 to 3, as said below
Outputs:
- field: float32 [8, 2, 32, 1024], P(('parts', 'ship'), None, None, 'panel'), parts along dimension 0
There are 2 independent parts, one for each index of `parts`. A program takes and returns all parts, laid end to end along the dimension named above; an argument that names none is the same for every part. Nothing has to cross between parts.
Inputs may be any that keep to these rules, and one draw needn't show every extreme that they name: Each row is a pairing of the ships: plan[k, plan[k, s]] = s and plan[k, s] != s; every two ships are paired in exactly one round. `near_columns`: the entries of one block row are distinct and differ from the row's own block.
All inputs are finite; a program needn't handle non-finite values.
Results may differ from a plain program's by a relative error of at most 0.0046.
Values may be sent and summed in bfloat16 or wider, within the bound.
A program may use at most 64 MiB of HBM per device.

v0:
```python
import jax
import jax.numpy as jnp
from jax import lax
from jax.sharding import PartitionSpec as P


def pair_up(product, rhs_count):
    real_src = product[:, :rhs_count]
    imag_src = product[:, rhs_count:]
    return jnp.stack([real_src[0] - imag_src[1], imag_src[0] + real_src[1]])


def near_field(values, columns, gathered):
    rhs_count = gathered.shape[1]
    block_len = values.shape[-1]
    cell_rows = gathered.reshape(2 * rhs_count, -1, block_len)
    picked = jnp.take(cell_rows, columns, axis=1)
    product = jnp.einsum("cinu,inztu->zcit", picked, values, preferred_element_type=jnp.float32)
    return pair_up(product, rhs_count).reshape(2, rhs_count, -1)


def apply_inverse(inverse, rest):
    rhs_count = rest.shape[1]
    block_len = inverse.shape[-1]
    rounded = rest.astype(jnp.bfloat16).reshape(2 * rhs_count, -1, block_len)
    product = jnp.einsum("ciu,iztu->zcit", rounded, inverse, preferred_element_type=jnp.float32)
    return pair_up(product, rhs_count).reshape(2, rhs_count, -1)


def compress(right_basis, sent):
    rhs_count = sent.shape[1]
    flat = sent.reshape(2 * rhs_count, -1)
    grams = jnp.einsum("zan,cn->zac", right_basis, flat, preferred_element_type=jnp.float32)
    return jnp.stack(
        [
            grams[0, :, :rhs_count] - grams[1, :, rhs_count:],
            grams[0, :, rhs_count:] + grams[1, :, :rhs_count],
        ]
    )


def expand(received, left_basis):
    outer = jnp.einsum("yac,zan->yzcn", received, left_basis, preferred_element_type=jnp.float32)
    return jnp.stack([outer[0, 0] - outer[1, 1], outer[0, 1] + outer[1, 0]])


def on_device(
    right_side,
    current,
    near_values,
    near_columns,
    block_inverse,
    coupling_right,
    coupling_left,
    pair_rank,
    plan,
):
    gathered = lax.all_gather(current[0], "panel", axis=2, tiled=True)
    rest = right_side[0] - near_field(near_values[0], near_columns[0], gathered)
    iterate = apply_inverse(block_inverse[0], rest)
    own_ship = lax.axis_index("ship")
    ship_count = coupling_left.shape[1]
    rank_index = lax.iota(jnp.int32, coupling_left.shape[3])
    for round_index in range(plan.shape[0]):
        partner = plan[round_index, own_ship]
        right_basis = lax.dynamic_index_in_dim(coupling_right, partner, 0, keepdims=False)[0]
        partial_value = compress(right_basis, iterate.astype(jnp.bfloat16))
        slot_mask = (lax.iota(jnp.int32, ship_count) == partner).astype(jnp.float32)
        spread = slot_mask[:, None, None, None] * partial_value[None]
        summed = lax.psum(spread, ("ship", "panel"))
        incoming = lax.dynamic_index_in_dim(summed, own_ship, 0, keepdims=False)
        keep_mask = rank_index < pair_rank[own_ship, partner]
        received = jnp.where(keep_mask[None, :, None], incoming, jnp.float32(0.0)).astype(
            jnp.bfloat16
        )
        left_basis = lax.dynamic_index_in_dim(coupling_left[0], partner, 0, keepdims=False)
        rest = rest - expand(received, left_basis)
        iterate = apply_inverse(block_inverse[0], rest)
    return iterate[None]


def solution(mesh):
    placed = (
        P(("parts", "ship"), None, None, "panel"),
        P(("parts", "ship"), None, None, "panel"),
        P(("parts", "ship"), "panel", None, None, None, None),
        P(("parts", "ship"), "panel", None),
        P(("parts", "ship"), "panel", None, None, None),
        P("parts", "ship", None, None, "panel"),
        P(("parts", "ship"), None, None, None, "panel"),
        P(),
        P(),
    )
    return jax.shard_map(
        on_device,
        mesh=mesh,
        in_specs=placed,
        out_specs=P(("parts", "ship"), None, None, "panel"),
        check_vma=False,
    )
```

profile of v0, /device:TPU:0, one launch (start us, length us, event | category | flops | bytes accessed | tf_op | source)
XLA Modules:
  0.0 216.4 jit_solution(11564814818696903876)
XLA Ops:
  0.0 1.4 constant_dynamic-slice_fusion.1
  7.0 0.7 fusion.72
  7.6 0.5 iota_compare_fusion.2
  8.2 15.1 %all-gather = bf16[1,2,32,1024]{3,2,1,0:T(8,128)(2,1)S(1)} all-gather(bf16[1,2,32,256]{3,2,1,0:T(8,128)(2,1)S(1)} %copy-done.5), channel_id=2, replica_groups=mesh['parts'=2,'ship'=4,'panel'=4] {'panel'}, dimensions={3}, use_global_device_ids=true | all-gather | bytes 163840 | tf_op jit(solution)/shard_map/all_gather | solution.py:58
  23.3 0.6 copy-done.7
  24.0 0.1 reshape.255
  24.1 0.6 gather_fusion
  24.7 0.4 convolution_bitcast_fusion
  25.3 0.8 copy-done.4
  26.2 0.8 copy-done.1
  27.0 0.2 convolution_bitcast_fusion.4
  27.2 0.7 copy-done.2
  28.0 0.1 fusion.16
  28.2 0.6 compare_convert_fusion.2
  28.8 0.1 broadcast_multiply_fusion.2
  28.9 60.9 %psum.21 = bf16[4,2,64,32]{2,3,1,0:T(8,128)(2,1)S(1)} all-reduce(f32[4,2,64,32]{2,3,1,0:T(8,128)S(1)} %broadcast_multiply_fusion.2), channel_id=1, replica_groups=mesh['parts'=2,'ship'=4,'panel'=4] {'ship','panel'}, use_global_device_ids=true, to_apply=%region_0.1 | all-reduce | flops 16384 | bytes 98304 | tf_op jit(solution)/shard_map/psum | solution.py:70
  89.8 0.1 convolution_bitcast_fusion.7
  90.1 0.2 convolution_bitcast_fusion.3
  90.3 0.1 fusion.14
  90.5 0.6 compare_convert_fusion.1
  91.2 0.1 broadcast_multiply_fusion.1
  91.2 60.0 %psum.22 = bf16[4,2,64,32]{2,3,1,0:T(8,128)(2,1)S(1)} all-reduce(f32[4,2,64,32]{2,3,1,0:T(8,128)S(1)} %broadcast_multiply_fusion.1), channel_id=1, replica_groups=mesh['parts'=2,'ship'=4,'panel'=4] {'ship','panel'}, use_global_device_ids=true, to_apply=%region_1.2 | all-reduce | flops 16384 | bytes 98304 | tf_op jit(solution)/shard_map/psum | solution.py:70
  151.2 0.6 iota_compare_fusion.1
  151.8 0.1 convolution_bitcast_fusion.6
  152.1 0.2 convolution_bitcast_fusion.2
  152.4 0.1 fusion.12
  152.6 0.7 compare_convert_fusion
  153.3 61.3 %psum.23 = bf16[4,2,64,32]{2,3,1,0:T(8,128)(2,1)S(1)} all-reduce(f32[4,2,64,32]{2,3,1,0:T(8,128)S(1)} %broadcast_multiply_fusion), channel_id=1, replica_groups=mesh['parts'=2,'ship'=4,'panel'=4] {'ship','panel'}, use_global_device_ids=true, to_apply=%region_2.3 | all-reduce | flops 16384 | bytes 98304 | tf_op jit(solution)/shard_map/psum | solution.py:70
  214.6 0.6 iota_compare_fusion
  215.2 0.1 convolution_bitcast_fusion.5
  215.5 0.2 convolution_bitcast_fusion.1
  215.8 0.6 copy.68
  (62 shorter events, 1.1 us)
Async XLA Ops:
  0.0 24.7 %copy-start = (bf16[1,2,6,2,128,128]{5,4,3,2,1,0:T(8,128)(2,1)S(1)}, bf16[1,2,6,2,128,128]{5,4,3,2,1,0:T(8,128)(2,1)}, u32[]{:S(2)}) copy-start(bf16[1,2,6,2,128,128]{5,4,3,2,1,0:T(8,128)(2,1)} %param.11) | copy-start | bytes 2359300
  0.0 8.2 %copy-start.5 = (bf16[1,2,32,256]{3,2,1,0:T(8,128)(2,1)S(1)}, bf16[1,2,32,256]{3,2,1,0:T(8,128)(2,1)}, u32[]{:S(2)}) copy-start(bf16[1,2,32,256]{3,2,1,0:T(8,128)(2,1)} %param.10) | copy-start | bytes 98308
  5.6 1.3 copy-start.6
  23.3 0.7 copy-start.7
  25.2 0.8 copy-start.4
  26.1 0.9 copy-start.1
  27.0 0.9 copy-start.2
  28.1 61.7 %copy-start.3 = (bf16[1,4,2,64,256]{4,3,2,1,0:T(8,128)(2,1)S(1)}, bf16[1,4,2,64,256]{4,3,2,1,0:T(8,128)(2,1)}, u32[]{:S(2)}) copy-start(bf16[1,4,2,64,256]{4,3,2,1,0:T(8,128)(2,1)} %param.15) | copy-start | bytes 786436
where the time goes:
time: 217 us; the launch traced here: 216 us
  blocking collectives  197 us (91%)
  local copies, waits for them, and re-layouts  6.77 us (3%)
  between operations  6.03 us (3%)
  other arithmetic  4.55 us (2%)
    psum x3, blocking collectives, on_device(): summed = lax.psum(spread, ('ship', 'panel'))  182 us
    all_gather x1, blocking collectives, on_device(): gathered = lax.all_gather(current[0], 'panel', axis=2, tiled=True)  15.1 us

commit v1 on v0

--- a/solution.py
+++ b/solution.py
@@ -1,7 +1,281 @@
+import functools
+import itertools
+
 import jax
 import jax.numpy as jnp
 from jax import lax
+from jax.experimental import pallas as pl
+from jax.experimental.pallas import tpu as pltpu
 from jax.sharding import PartitionSpec as P
+
+BF16 = jnp.bfloat16
+F32 = jnp.float32
+
+
+def dot_nt(a, b):
+    return lax.dot_general(a, b, (((1,), (1,)), ((), ())), preferred_element_type=F32)
+
+
+def dot_nn(a, b):
+    return lax.dot_general(a, b, (((1,), (0,)), ((), ())), preferred_element_type=F32)
+
+
+def partner_of(ship, match):
+    if match == 1:
+        return ship + 1 - 2 * (ship % 2)
+    if match == 2:
+        return ship + 2 - 4 * (ship // 2)
+    return 3 - ship
+
+
+def complex_pair(product, rows, cols):
+    real = product[:rows, :cols] - product[rows:, cols:]
+    imag = product[rows:, :cols] + product[:rows, cols:]
+    return real, imag
+
+
+def sweep_kernel(
+    order,
+    panels,
+    near_columns,
+    pair_rank,
+    right_side,
+    current,
+    near_values,
+    block_inverse,
+    coupling_right,
+    coupling_left,
+    field,
+    ring,
+    side,
+    values,
+    inverse,
+    right,
+    left,
+    outbox,
+    slots,
+    load_sem,
+    gather_send,
+    gather_recv,
+    round_send,
+    round_recv,
+):
+    ship = lax.axis_index("ship")
+    panel = lax.axis_index("panel")
+    blocks, terms = near_values.shape[1], near_values.shape[2]
+    block = near_values.shape[-1]
+    rhs = current.shape[2]
+    rank = coupling_left.shape[3]
+    rounds = len(order)
+    partners = [partner_of(ship, match) for match in order]
+
+    barrier = pltpu.get_barrier_semaphore()
+    for step in range(1, panels):
+        pl.semaphore_signal(
+            barrier,
+            inc=1,
+            device_id={"panel": (panel + step) % panels},
+            device_id_type=pl.DeviceIdType.MESH,
+        )
+    for partner in partners:
+        for target in range(panels):
+            pl.semaphore_signal(
+                barrier,
+                inc=1,
+                device_id={"ship": partner, "panel": target},
+                device_id_type=pl.DeviceIdType.MESH,
+            )
+
+    own = [
+        pltpu.make_async_copy(
+            current.at[0, :, :, b * block : (b + 1) * block],
+            ring.at[panel * blocks + b],
+            load_sem.at[b],
+        )
+        for b in range(blocks)
+    ]
+    bases = [
+        pltpu.make_async_copy(block_inverse.at[0], inverse, load_sem.at[blocks]),
+        pltpu.make_async_copy(coupling_left.at[0], left, load_sem.at[blocks + 1]),
+        pltpu.make_async_copy(coupling_right, right, load_sem.at[blocks + 2]),
+    ]
+    near_loads = [
+        pltpu.make_async_copy(right_side.at[0], side, load_sem.at[blocks + 3]),
+        pltpu.make_async_copy(near_values.at[0], values, load_sem.at[blocks + 4]),
+    ]
+    for copy in own + bases + near_loads:
+        copy.start()
+    for copy in own:
+        copy.wait()
+
+    pl.semaphore_wait(barrier, panels - 1 + rounds * panels)
+    mine = ring.at[pl.ds(panel * blocks, blocks)]
+    spread = [
+        pltpu.make_async_remote_copy(
+            src_ref=mine,
+            dst_ref=mine,
+            send_sem=gather_send.at[step - 1],
+            recv_sem=gather_recv.at[step - 1],
+            device_id={"panel": (panel + step) % panels},
+            device_id_type=pl.DeviceIdType.MESH,
+        )
+        for step in range(1, panels)
+    ]
+    for copy in spread:
+        copy.start()
+
+    for copy in bases:
+        copy.wait()
+    inv = [inverse[b].reshape(2 * block, block) for b in range(blocks)]
+    raw = [left[p] for p in partners]
+    moved = []
+    for b in range(blocks):
+        rows = jnp.concatenate(
+            [r[y, :, b * block : (b + 1) * block] for y in range(2) for r in raw], axis=0
+        )
+        moved.append(complex_pair(dot_nt(rows, inv[b]), rounds * rank, block))
+    moved_re = jnp.concatenate([m[0] for m in moved], axis=1)
+    moved_im = jnp.concatenate([m[1] for m in moved], axis=1)
+    spreaders = []
+    for k in range(rounds):
+        re, im = moved_re[k * rank : (k + 1) * rank], moved_im[k * rank : (k + 1) * rank]
+        spreaders.append(
+            jnp.concatenate(
+                [jnp.concatenate([re, im], axis=1), jnp.concatenate([-im, re], axis=1)], axis=0
+            ).astype(BF16)
+        )
+    gatherers = []
+    for p in partners:
+        re, im = right[p, 0, 0], right[p, 0, 1]
+        gatherers.append(
+            jnp.concatenate(
+                [jnp.concatenate([re, -im], axis=1), jnp.concatenate([im, re], axis=1)], axis=0
+            )
+        )
+    links = {
+        (k, j): dot_nt(spreaders[j], gatherers[k]).astype(BF16)
+        for k in range(rounds)
+        for j in range(k)
+    }
+
+    for copy in near_loads:
+        copy.wait()
+    for copy in spread:
+        copy.wait_recv()
+
+    start_re, start_im = [], []
+    for b in range(blocks):
+        picked = jnp.concatenate(
+            [ring[near_columns[0, b, n]].reshape(2 * rhs, block) for n in range(terms)], axis=1
+        )
+        weights = jnp.concatenate(
+            [values[b, n].reshape(2 * block, block) for n in range(terms)], axis=1
+        )
+        re, im = complex_pair(dot_nt(picked, weights), rhs, block)
+        cols = slice(b * block, (b + 1) * block)
+        rest = jnp.concatenate([side[0, :, cols] - re, side[1, :, cols] - im], axis=0)
+        re, im = complex_pair(dot_nt(rest.astype(BF16), inv[b]), rhs, block)
+        start_re.append(re)
+        start_im.append(im)
+    total = jnp.concatenate(start_re + start_im, axis=1)
+    sent = total.astype(BF16)
+    parts = [dot_nt(sent, g) for g in gatherers]
+
+    lane = lax.broadcasted_iota(jnp.int32, (rhs, 2 * rank), 1)
+    lane = jnp.where(lane < rank, lane, lane - rank)
+    flights = []
+    for k in range(rounds):
+        outbox[k] = parts[k].astype(BF16)
+        copies = [
+            pltpu.make_async_remote_copy(
+                src_ref=outbox.at[k],
+                dst_ref=slots.at[k, step],
+                send_sem=round_send.at[k, step],
+                recv_sem=round_recv.at[k, step],
+                device_id={"ship": partners[k], "panel": (panel + step) % panels},
+                device_id_type=pl.DeviceIdType.MESH,
+            )
+            for step in range(panels)
+        ]
+        for copy in copies:
+            copy.start()
+        flights += copies
+        if k > 0:
+            total = total - dot_nn(received, spreaders[k - 1])
+            for later in range(k + 1, rounds):
+                parts[later] = parts[later] - dot_nn(received, links[later, k - 1])
+        for copy in copies:
+            copy.wait_recv()
+        summed = slots[k, 0].astype(F32)
+        for source in range(1, panels):
+            summed = summed + slots[k, source].astype(F32)
+        kept = pair_rank[ship, partners[k]]
+        received = jnp.where(lane < kept, summed, 0.0).astype(BF16)
+        if k + 1 < rounds:
+            parts[k + 1] = parts[k + 1] - dot_nn(received, links[k + 1, k])
+    total = total - dot_nn(received, spreaders[rounds - 1])
+    width = blocks * block
+    field[0, 0] = total[:, :width]
+    field[0, 1] = total[:, width:]
+    for copy in spread + flights:
+        copy.wait_send()
+
+
+def sweep_call(order, collective_id, panels, operands):
+    (right_side, current, near_values, near_columns, block_inverse, coupling_right, coupling_left, pair_rank) = operands
+    blocks = near_values.shape[1]
+    block = near_values.shape[-1]
+    rhs = current.shape[2]
+    rank = coupling_left.shape[3]
+    rounds = len(order)
+    anywhere = pl.BlockSpec(memory_space=pl.ANY)
+    scalars = pl.BlockSpec(memory_space=pltpu.SMEM)
+    return pl.pallas_call(
+        functools.partial(sweep_kernel, order, panels),
+        out_shape=jax.ShapeDtypeStruct(right_side.shape, F32),
+        in_specs=[scalars, scalars] + [anywhere] * 6,
+        out_specs=pl.BlockSpec(memory_space=pltpu.VMEM),
+        scratch_shapes=[
+            pltpu.VMEM((panels * blocks, 2, rhs, block), BF16),
+            pltpu.VMEM(right_side.shape[1:], F32),
+            pltpu.VMEM(near_values.shape[1:], BF16),
+            pltpu.VMEM(block_inverse.shape[1:], BF16),
+            pltpu.VMEM(coupling_right.shape, BF16),
+            pltpu.VMEM(coupling_left.shape[1:], BF16),
+            pltpu.VMEM((rounds, rhs, 2 * rank), BF16),
+            pltpu.VMEM((rounds, panels, rhs, 2 * rank), BF16),
+            pltpu.SemaphoreType.DMA((blocks + 5,)),
+            pltpu.SemaphoreType.DMA((panels - 1,)),
+            pltpu.SemaphoreType.DMA((panels - 1,)),
+            pltpu.SemaphoreType.DMA((rounds, panels)),
+            pltpu.SemaphoreType.DMA((rounds, panels)),
+        ],
+        compiler_params=pltpu.CompilerParams(
+            collective_id=collective_id,
+            has_side_effects=True,
+            vmem_limit_bytes=24 * 1024 * 1024,
+        ),
+    )(
+        near_columns,
+        pair_rank,
+        right_side,
+        current,
+        near_values,
+        block_inverse,
+        coupling_right,
+        coupling_left,
+    )
+
+
+def four_ships(panels, right_side, current, near_values, near_columns, block_inverse, coupling_right, coupling_left, pair_rank, plan):
+    orders = list(itertools.permutations((1, 2, 3)))
+    index = 2 * (plan[0, 0] - 1) + (plan[1, 0] > plan[2, 0]).astype(jnp.int32)
+    operands = (right_side, current, near_values, near_columns, block_inverse, coupling_right, coupling_left, pair_rank)
+    branches = [
+        functools.partial(lambda order, number, *args: sweep_call(order, number, panels, args), order, number)
+        for number, order in enumerate(orders)
+    ]
+    return lax.switch(index, branches, *operands)
 
 
 def pair_up(product, rhs_count):
@@ -14,7 +288,19 @@
     rhs_count = gathered.shape[1]
     block_len = values.shape[-1]
     cell_rows = gathered.reshape(2 * rhs_count, -1, block_len)
-    picked = jnp.take(cell_rows, columns, axis=1)
+    picked = jnp.stack(
+        [
+            jnp.stack(
+                [
+                    lax.dynamic_index_in_dim(cell_rows, columns[i, n], 1, keepdims=False)
+                    for n in range(columns.shape[1])
+                ],
+                axis=1,
+            )
+            for i in range(columns.shape[0])
+        ],
+        axis=1,
+    )
     product = jnp.einsum("cinu,inztu->zcit", picked, values, preferred_element_type=jnp.float32)
     return pair_up(product, rhs_count).reshape(2, rhs_count, -1)
 
@@ -44,7 +330,7 @@
     return jnp.stack([outer[0, 0] - outer[1, 1], outer[0, 1] + outer[1, 0]])
 
 
-def on_device(
+def any_ships(
     right_side,
     current,
     near_values,
@@ -91,6 +377,8 @@
         P(),
         P(),
     )
+    ships, panels = mesh.shape["ship"], mesh.shape["panel"]
+    on_device = functools.partial(four_ships, panels) if ships == 4 and panels <= 8 else any_ships
     return jax.shard_map(
         on_device,
         mesh=mesh,

time: 217 us -> 28.1 us (0.13)
  blocking collectives: 197 us -> 0 us
  Pallas kernels: 0 us -> 23.3 us
  other arithmetic: 4.55 us -> 0 us
  local copies, waits for them, and re-layouts: 6.77 us -> 2.67 us
  between operations: 6.03 us -> 1.94 us
    psum x3 -> x0, blocking collectives: 182 us -> none  [on_device(): summed = lax.psum(spread, ('ship', 'panel'))]
    pallas_call x0 -> x1, Pallas kernels: none -> 23.3 us  [sweep_call(): pl.pallas_call(functools.partial(sweep_kernel, order, panels), out_shape=...]
    all_gather x1 -> x0, blocking collectives: 15.1 us -> none  [on_device(): gathered = lax.all_gather(current[0], 'panel', axis=2, tiled=True)]
where the time goes in v1:
time: 28.1 us; the launch traced here: 28 us
  Pallas kernels  23.3 us (83%)
  local copies, waits for them, and re-layouts  2.67 us (10%)
  between operations  1.94 us (7%)
    pallas_call x1, Pallas kernels, sweep_call(): pl.pallas_call(functools.partial(sweep_kernel, order, panels), out_shape=...  23.3 us
    slice x1, local copies, waits for them, and re-layouts, four_ships(): index = 2 * (plan[0, 0] - 1) + (plan[1, 0] > plan[2, 0]).astype(jnp.int32)  1.36 us
    unnamed x5, local copies, waits for them, and re-layouts  1.31 us

profile of v1, /device:TPU:0, one launch (start us, length us, event | category | flops | bytes accessed | tf_op | source)
XLA Modules:
  0.0 28.0 jit_solution(15252017206877359197)
XLA Ops:
  0.0 1.4 %fusion = (s32[1,1]{1,0:T(1,128)}, s32[1,1]{1,0:T(1,128)}, s32[1,1]{1,0:T(1,128)}) fusion(s32[3,4]{1,0:T(4,128)} %param.23), kind=kLoop, calls=%fused_computation | loop fusion | bytes 24 | tf_op jit(solution)/shard_map/slice | solution.py:272
  3.3 0.0 copy-start
  3.3 0.0 copy-start.1
  3.3 0.7 %copy-done = s32[4,4]{1,0:T(4,128)S(1)} copy-done((s32[4,4]{1,0:T(4,128)S(1)}, s32[4,4]{1,0:T(4,128)}, u32[]{:S(2)}) %copy-start) | copy-done | bytes 88
  4.0 0.0 copy-done.1
  4.0 23.4 %conditional.1 = (f32[1,2,32,256]{3,2,1,0:T(8,128)S(1)}) conditional(s32[]{:T(128)} %bitcast, (s32[1,2,6]{2,1,0:T(2,128)S(1)}, s32[4,4]{1,0:T(4,128)S(1)}, f32[1,2,32,256]{3,2,1,0:T(8,128)}, bf16[1,2,32,256]{3,2,1,0:T(8,128)(2,1)}, bf16[1,2,6,2,128,128]{5,4,3,2,1,0:T(8,128)(2,1)}, ...), branch_computations={%region_0.0_spmd, %region_1.0_spmd, %region_2.0_spmd, %region_3.0_... | conditional | bytes 8 | solution.py:278
  4.0 23.3 %branch_0_fun.1 = f32[1,2,32,256]{3,2,1,0:T(8,128)S(1)} custom-call(s32[1,2,6]{2,1,0:T(2,128)S(1)} %get-tuple-element.96.near_columns, s32[4,4]{1,0:T(4,128)S(1)} %get-tuple-element.98.pair_rank, f32[1,2,32,256]{3,2,1,0:T(8,128)} %get-tuple-element.108.right_side, bf16[1,2,32,256]{3,2,1,0:T(8,128)(2,1)} %get-tuple-element.110.current, ...), custom_call_target="tpu_custom_call" | custom-call | tf_op jit(solution)/shard_map/cond/branch_0_fun/pallas_call | solution.py:233
  27.3 0.6 %copy.23 = f32[1,2,32,256]{3,2,1,0:T(8,128)} copy(f32[1,2,32,256]{3,2,1,0:T(8,128)S(1)} %get-tuple-element.156) | data formatting | bytes 131072
Async XLA Ops:
  3.3 0.7 %copy-start = (s32[4,4]{1,0:T(4,128)S(1)}, s32[4,4]{1,0:T(4,128)}, u32[]{:S(2)}) copy-start(s32[4,4]{1,0:T(4,128)} %param.22) | copy-start | bytes 196
  3.3 0.7 %copy-start.1 = (s32[1,2,6]{2,1,0:T(2,128)S(1)}, s32[1,2,6]{2,1,0:T(2,128)}, u32[]{:S(2)}) copy-start(s32[1,2,6]{2,1,0:T(2,128)} %param.18) | copy-start | bytes 148

commit v2 on v1

--- a/solution.py
+++ b/solution.py
@@ -1,5 +1,4 @@
 import functools
-import itertools
 
 import jax
 import jax.numpy as jnp
@@ -20,25 +19,24 @@
     return lax.dot_general(a, b, (((1,), (0,)), ((), ())), preferred_element_type=F32)
 
 
-def partner_of(ship, match):
-    if match == 1:
-        return ship + 1 - 2 * (ship % 2)
-    if match == 2:
-        return ship + 2 - 4 * (ship // 2)
-    return 3 - ship
-
-
 def complex_pair(product, rows, cols):
     real = product[:rows, :cols] - product[rows:, cols:]
     imag = product[rows:, :cols] + product[:rows, cols:]
     return real, imag
 
 
+def times_i(real, imag):
+    return jnp.concatenate(
+        [jnp.concatenate([real, imag], axis=1), jnp.concatenate([-imag, real], axis=1)], axis=0
+    )
+
+
 def sweep_kernel(
-    order,
+    ships,
     panels,
-    near_columns,
-    pair_rank,
+    columns_hbm,
+    rank_hbm,
+    plan_hbm,
     right_side,
     current,
     near_values,
@@ -46,19 +44,26 @@
     coupling_right,
     coupling_left,
     field,
+    near_columns,
+    pair_rank,
+    plan,
     ring,
     side,
     values,
     inverse,
     right,
     left,
-    outbox,
-    slots,
+    link_out,
+    link_in,
+    all_links,
+    part_out,
+    part_in,
+    all_parts,
     load_sem,
-    gather_send,
-    gather_recv,
-    round_send,
-    round_recv,
+    panel_send,
+    panel_recv,
+    ship_send,
+    ship_recv,
 ):
     ship = lax.axis_index("ship")
     panel = lax.axis_index("panel")
@@ -66,8 +71,34 @@
     block = near_values.shape[-1]
     rhs = current.shape[2]
     rank = coupling_left.shape[3]
-    rounds = len(order)
-    partners = [partner_of(ship, match) for match in order]
+    rounds = plan.shape[0]
+    pairs = [(k, j) for k in range(rounds) for j in range(k)]
+
+    def to_panels(stage, source, target):
+        return [
+            pltpu.make_async_remote_copy(
+                src_ref=source(step),
+                dst_ref=target(step),
+                send_sem=panel_send.at[stage, step - 1],
+                recv_sem=panel_recv.at[stage, step - 1],
+                device_id={"panel": (panel + step) % panels},
+                device_id_type=pl.DeviceIdType.MESH,
+            )
+            for step in range(1, panels)
+        ]
+
+    def to_ships(stage, ref):
+        return [
+            pltpu.make_async_remote_copy(
+                src_ref=ref,
+                dst_ref=ref,
+                send_sem=ship_send.at[stage, step - 1],
+                recv_sem=ship_recv.at[stage, step - 1],
+                device_id={"ship": (ship + step) % ships},
+                device_id_type=pl.DeviceIdType.MESH,
+            )
+            for step in range(1, ships)
+        ]
 
     barrier = pltpu.get_barrier_semaphore()
     for step in range(1, panels):
@@ -77,14 +108,13 @@
             device_id={"panel": (panel + step) % panels},
             device_id_type=pl.DeviceIdType.MESH,
         )
-    for partner in partners:
-        for target in range(panels):
-            pl.semaphore_signal(
-                barrier,
-                inc=1,
-                device_id={"ship": partner, "panel": target},
-                device_id_type=pl.DeviceIdType.MESH,
-            )
+    for step in range(1, ships):
+        pl.semaphore_signal(
+            barrier,
+            inc=1,
+            device_id={"ship": (ship + step) % ships},
+            device_id_type=pl.DeviceIdType.MESH,
+        )
 
     own = [
         pltpu.make_async_copy(
@@ -95,37 +125,31 @@
         for b in range(blocks)
     ]
     bases = [
-        pltpu.make_async_copy(block_inverse.at[0], inverse, load_sem.at[blocks]),
-        pltpu.make_async_copy(coupling_left.at[0], left, load_sem.at[blocks + 1]),
-        pltpu.make_async_copy(coupling_right, right, load_sem.at[blocks + 2]),
+        pltpu.make_async_copy(plan_hbm, plan, load_sem.at[blocks]),
+        pltpu.make_async_copy(block_inverse.at[0], inverse, load_sem.at[blocks + 1]),
+        pltpu.make_async_copy(coupling_left.at[0], left, load_sem.at[blocks + 2]),
+        pltpu.make_async_copy(coupling_right, right, load_sem.at[blocks + 3]),
     ]
     near_loads = [
-        pltpu.make_async_copy(right_side.at[0], side, load_sem.at[blocks + 3]),
-        pltpu.make_async_copy(near_values.at[0], values, load_sem.at[blocks + 4]),
+        pltpu.make_async_copy(columns_hbm, near_columns, load_sem.at[blocks + 4]),
+        pltpu.make_async_copy(rank_hbm, pair_rank, load_sem.at[blocks + 5]),
+        pltpu.make_async_copy(right_side.at[0], side, load_sem.at[blocks + 6]),
+        pltpu.make_async_copy(near_values.at[0], values, load_sem.at[blocks + 7]),
     ]
     for copy in own + bases + near_loads:
         copy.start()
     for copy in own:
         copy.wait()
 
-    pl.semaphore_wait(barrier, panels - 1 + rounds * panels)
+    pl.semaphore_wait(barrier, panels - 1 + ships - 1)
     mine = ring.at[pl.ds(panel * blocks, blocks)]
-    spread = [
-        pltpu.make_async_remote_copy(
-            src_ref=mine,
-            dst_ref=mine,
-            send_sem=gather_send.at[step - 1],
-            recv_sem=gather_recv.at[step - 1],
-            device_id={"panel": (panel + step) % panels},
-            device_id_type=pl.DeviceIdType.MESH,
-        )
-        for step in range(1, panels)
-    ]
+    spread = to_panels(0, lambda step: mine, lambda step: mine)
     for copy in spread:
         copy.start()
 
     for copy in bases:
         copy.wait()
+    partners = [plan[k, ship] for k in range(rounds)]
     inv = [inverse[b].reshape(2 * block, block) for b in range(blocks)]
     raw = [left[p] for p in partners]
     moved = []
@@ -138,12 +162,8 @@
     moved_im = jnp.concatenate([m[1] for m in moved], axis=1)
     spreaders = []
     for k in range(rounds):
-        re, im = moved_re[k * rank : (k + 1) * rank], moved_im[k * rank : (k + 1) * rank]
-        spreaders.append(
-            jnp.concatenate(
-                [jnp.concatenate([re, im], axis=1), jnp.concatenate([-im, re], axis=1)], axis=0
-            ).astype(BF16)
-        )
+        cut = slice(k * rank, (k + 1) * rank)
+        spreaders.append(times_i(moved_re[cut], moved_im[cut]).astype(BF16))
     gatherers = []
     for p in partners:
         re, im = right[p, 0, 0], right[p, 0, 1]
@@ -152,11 +172,16 @@
                 [jnp.concatenate([re, -im], axis=1), jnp.concatenate([im, re], axis=1)], axis=0
             )
         )
-    links = {
-        (k, j): dot_nt(spreaders[j], gatherers[k]).astype(BF16)
-        for k in range(rounds)
-        for j in range(k)
-    }
+    share = rank // panels
+    for index, (k, j) in enumerate(pairs):
+        link = dot_nt(spreaders[j][:rank], gatherers[k]).astype(BF16)
+        for target in range(panels):
+            link_out[target, index] = link[target * share : (target + 1) * share]
+    scatter = to_panels(
+        1, lambda step: link_out.at[(panel + step) % panels], lambda step: link_in.at[step - 1]
+    )
+    for copy in scatter:
+        copy.start()
 
     for copy in near_loads:
         copy.wait()
@@ -179,85 +204,111 @@
         start_im.append(im)
     total = jnp.concatenate(start_re + start_im, axis=1)
     sent = total.astype(BF16)
-    parts = [dot_nt(sent, g) for g in gatherers]
+    own_parts = [dot_nt(sent, g) for g in gatherers]
+    for k in range(rounds):
+        part_out[k] = own_parts[k].astype(BF16)
+    part_flight = to_panels(2, lambda step: part_out, lambda step: part_in.at[step - 1])
+    for copy in part_flight:
+        copy.start()
+
+    for copy in scatter:
+        copy.wait_recv()
+    for index in range(len(pairs)):
+        summed = link_out[panel, index].astype(F32)
+        for step in range(1, panels):
+            summed = summed + link_in[step - 1, index].astype(F32)
+        all_links[ship, panel, index] = summed.astype(BF16)
+    piece = all_links.at[ship, panel]
+    link_flight = to_panels(3, lambda step: piece, lambda step: piece)
+    for copy in link_flight:
+        copy.start()
+
+    for copy in part_flight:
+        copy.wait_recv()
+    for k in range(rounds):
+        summed = own_parts[k]
+        for step in range(1, panels):
+            summed = summed + part_in[step - 1, k].astype(F32)
+        all_parts[ship, k] = summed.astype(BF16)
+    part_ships = to_ships(0, all_parts.at[ship])
+    for copy in part_ships:
+        copy.start()
+    for copy in link_flight:
+        copy.wait_recv()
+    link_ships = to_ships(1, all_links.at[ship])
+    for copy in link_ships:
+        copy.start()
+    for copy in part_ships + link_ships:
+        copy.wait_recv()
 
     lane = lax.broadcasted_iota(jnp.int32, (rhs, 2 * rank), 1)
     lane = jnp.where(lane < rank, lane, lane - rank)
-    flights = []
+
+    def received(k, target, partner):
+        value = all_parts[partner, k].astype(F32)
+        for j in range(k):
+            index = pairs.index((k, j))
+            rows = jnp.concatenate(
+                [all_links[partner, q, index] for q in range(panels)], axis=0
+            ).astype(F32)
+            link = times_i(rows[:, :rank], rows[:, rank:]).astype(BF16)
+            value = value - dot_nn(received(j, partner, plan[j, partner]), link)
+        return jnp.where(lane < pair_rank[target, partner], value, 0.0).astype(BF16)
+
     for k in range(rounds):
-        outbox[k] = parts[k].astype(BF16)
-        copies = [
-            pltpu.make_async_remote_copy(
-                src_ref=outbox.at[k],
-                dst_ref=slots.at[k, step],
-                send_sem=round_send.at[k, step],
-                recv_sem=round_recv.at[k, step],
-                device_id={"ship": partners[k], "panel": (panel + step) % panels},
-                device_id_type=pl.DeviceIdType.MESH,
-            )
-            for step in range(panels)
-        ]
-        for copy in copies:
-            copy.start()
-        flights += copies
-        if k > 0:
-            total = total - dot_nn(received, spreaders[k - 1])
-            for later in range(k + 1, rounds):
-                parts[later] = parts[later] - dot_nn(received, links[later, k - 1])
-        for copy in copies:
-            copy.wait_recv()
-        summed = slots[k, 0].astype(F32)
-        for source in range(1, panels):
-            summed = summed + slots[k, source].astype(F32)
-        kept = pair_rank[ship, partners[k]]
-        received = jnp.where(lane < kept, summed, 0.0).astype(BF16)
-        if k + 1 < rounds:
-            parts[k + 1] = parts[k + 1] - dot_nn(received, links[k + 1, k])
-    total = total - dot_nn(received, spreaders[rounds - 1])
+        total = total - dot_nn(received(k, ship, partners[k]), spreaders[k])
     width = blocks * block
     field[0, 0] = total[:, :width]
     field[0, 1] = total[:, width:]
-    for copy in spread + flights:
+    for copy in spread + scatter + part_flight + link_flight + part_ships + link_ships:
         copy.wait_send()
 
 
-def sweep_call(order, collective_id, panels, operands):
-    (right_side, current, near_values, near_columns, block_inverse, coupling_right, coupling_left, pair_rank) = operands
+def few_ships(ships, panels, right_side, current, near_values, near_columns, block_inverse, coupling_right, coupling_left, pair_rank, plan):
     blocks = near_values.shape[1]
     block = near_values.shape[-1]
     rhs = current.shape[2]
     rank = coupling_left.shape[3]
-    rounds = len(order)
+    rounds = plan.shape[0]
+    links = rounds * (rounds - 1) // 2
+    share = rank // panels
     anywhere = pl.BlockSpec(memory_space=pl.ANY)
-    scalars = pl.BlockSpec(memory_space=pltpu.SMEM)
     return pl.pallas_call(
-        functools.partial(sweep_kernel, order, panels),
+        functools.partial(sweep_kernel, ships, panels),
         out_shape=jax.ShapeDtypeStruct(right_side.shape, F32),
-        in_specs=[scalars, scalars] + [anywhere] * 6,
+        in_specs=[anywhere] * 9,
         out_specs=pl.BlockSpec(memory_space=pltpu.VMEM),
         scratch_shapes=[
+            pltpu.SMEM(near_columns.shape, jnp.int32),
+            pltpu.SMEM(pair_rank.shape, jnp.int32),
+            pltpu.SMEM(plan.shape, jnp.int32),
             pltpu.VMEM((panels * blocks, 2, rhs, block), BF16),
             pltpu.VMEM(right_side.shape[1:], F32),
             pltpu.VMEM(near_values.shape[1:], BF16),
             pltpu.VMEM(block_inverse.shape[1:], BF16),
             pltpu.VMEM(coupling_right.shape, BF16),
             pltpu.VMEM(coupling_left.shape[1:], BF16),
+            pltpu.VMEM((panels, links, share, 2 * rank), BF16),
+            pltpu.VMEM((panels - 1, links, share, 2 * rank), BF16),
+            pltpu.VMEM((ships, panels, links, share, 2 * rank), BF16),
             pltpu.VMEM((rounds, rhs, 2 * rank), BF16),
-            pltpu.VMEM((rounds, panels, rhs, 2 * rank), BF16),
-            pltpu.SemaphoreType.DMA((blocks + 5,)),
-            pltpu.SemaphoreType.DMA((panels - 1,)),
-            pltpu.SemaphoreType.DMA((panels - 1,)),
-            pltpu.SemaphoreType.DMA((rounds, panels)),
-            pltpu.SemaphoreType.DMA((rounds, panels)),
+            pltpu.VMEM((panels - 1, rounds, rhs, 2 * rank), BF16),
+            pltpu.VMEM((ships, rounds, rhs, 2 * rank), BF16),
+            pltpu.SemaphoreType.DMA((blocks + 8,)),
+            pltpu.SemaphoreType.DMA((4, panels - 1)),
+            pltpu.SemaphoreType.DMA((4, panels - 1)),
+            pltpu.SemaphoreType.DMA((2, ships - 1)),
+            pltpu.SemaphoreType.DMA((2, ships - 1)),
         ],
         compiler_params=pltpu.CompilerParams(
-            collective_id=collective_id,
+            collective_id=0,
             has_side_effects=True,
-            vmem_limit_bytes=24 * 1024 * 1024,
+            vmem_limit_bytes=60 * 1024 * 1024,
         ),
     )(
         near_columns,
         pair_rank,
+        plan,
         right_side,
         current,
         near_values,
@@ -265,17 +316,6 @@
         coupling_right,
         coupling_left,
     )
-
-
-def four_ships(panels, right_side, current, near_values, near_columns, block_inverse, coupling_right, coupling_left, pair_rank, plan):
-    orders = list(itertools.permutations((1, 2, 3)))
-    index = 2 * (plan[0, 0] - 1) + (plan[1, 0] > plan[2, 0]).astype(jnp.int32)
-    operands = (right_side, current, near_values, near_columns, block_inverse, coupling_right, coupling_left, pair_rank)
-    branches = [
-        functools.partial(lambda order, number, *args: sweep_call(order, number, panels, args), order, number)
-        for number, order in enumerate(orders)
-    ]
-    return lax.switch(index, branches, *operands)
 
 
 def pair_up(product, rhs_count):
@@ -378,7 +418,7 @@
         P(),
     )
     ships, panels = mesh.shape["ship"], mesh.shape["panel"]
-    on_device = functools.partial(four_ships, panels) if ships == 4 and panels <= 8 else any_ships
+    on_device = functools.partial(few_ships, ships, panels) if ships == 4 and panels == 4 else any_ships
     return jax.shard_map(
         on_device,
         mesh=mesh,

time: 28.1 us -> 22.2 us (0.79)
  Pallas kernels: 23.3 us -> 20.6 us
  between operations: 1.94 us -> 0.01 us
  local copies, waits for them, and re-layouts: 2.67 us -> 1.47 us
    pallas_call x1, Pallas kernels: 23.3 us -> 20.6 us  [few_ships(): pl.pallas_call(functools.partial(sweep_kernel, ships, panels), out_shape=...]
    slice x1 -> x0, local copies, waits for them, and re-layouts: 1.36 us -> none  [four_ships(): index = 2 * (plan[0, 0] - 1) + (plan[1, 0] > plan[2, 0]).astype(jnp.int32)]
    unnamed x5 -> x1, local copies, waits for them, and re-layouts: 1.31 us -> 1.47 us
where the time goes in v2:
time: 22.2 us; the launch traced here: 22.1 us
  Pallas kernels  20.6 us (93%)
  local copies, waits for them, and re-layouts  1.47 us (7%)
    pallas_call x1, Pallas kernels, few_ships(): pl.pallas_call(functools.partial(sweep_kernel, ships, panels), out_shape=...  20.6 us
    unnamed x1, local copies, waits for them, and re-layouts  1.47 us

profile of v2, /device:TPU:0, one launch (start us, length us, event | category | flops | bytes accessed | tf_op | source)
XLA Modules:
  0.0 22.1 jit_solution(16851795426934961335)
XLA Ops:
  0.0 20.6 %shard_map.91 = f32[1,2,32,256]{3,2,1,0:T(8,128)} custom-call(s32[1,2,6]{2,1,0:T(2,128)} %columns_hbm.1, s32[4,4]{1,0:T(4,128)} %rank_hbm.1, s32[3,4]{1,0:T(4,128)} %plan_hbm.1, f32[1,2,32,256]{3,2,1,0:T(8,128)} %right_side.1, bf16[1,2,32,256]{3,2,1,0:T(8,128)(2,1)} %current.1, bf16[1,2,6,2,128,128]{5,4,3,2,1,0:T(8,128)(2,1)} %near_values.1, ...), custom_call_target="tpu_custom_call" | custom-call | tf_op jit(solution)/shard_map/pallas_call | solution.py:276
  20.6 1.5 %copy.11 = f32[1,2,32,256]{3,2,1,0:T(8,128)} copy(f32[1,2,32,256]{3,2,1,0:T(8,128)} %shard_map.91) | data formatting | bytes 131072

commit v3 on v2

--- a/solution.py
+++ b/solution.py
@@ -116,34 +116,24 @@
             device_id_type=pl.DeviceIdType.MESH,
         )
 
-    own = [
-        pltpu.make_async_copy(
-            current.at[0, :, :, b * block : (b + 1) * block],
-            ring.at[panel * blocks + b],
-            load_sem.at[b],
-        )
-        for b in range(blocks)
-    ]
+    own = pltpu.make_async_copy(current.at[0], ring.at[panel], load_sem.at[8])
     bases = [
-        pltpu.make_async_copy(plan_hbm, plan, load_sem.at[blocks]),
-        pltpu.make_async_copy(block_inverse.at[0], inverse, load_sem.at[blocks + 1]),
-        pltpu.make_async_copy(coupling_left.at[0], left, load_sem.at[blocks + 2]),
-        pltpu.make_async_copy(coupling_right, right, load_sem.at[blocks + 3]),
+        pltpu.make_async_copy(plan_hbm, plan, load_sem.at[0]),
+        pltpu.make_async_copy(block_inverse.at[0], inverse, load_sem.at[1]),
+        pltpu.make_async_copy(coupling_left.at[0], left, load_sem.at[2]),
+        pltpu.make_async_copy(coupling_right, right, load_sem.at[3]),
     ]
     near_loads = [
-        pltpu.make_async_copy(columns_hbm, near_columns, load_sem.at[blocks + 4]),
-        pltpu.make_async_copy(rank_hbm, pair_rank, load_sem.at[blocks + 5]),
-        pltpu.make_async_copy(right_side.at[0], side, load_sem.at[blocks + 6]),
-        pltpu.make_async_copy(near_values.at[0], values, load_sem.at[blocks + 7]),
+        pltpu.make_async_copy(columns_hbm, near_columns, load_sem.at[4]),
+        pltpu.make_async_copy(rank_hbm, pair_rank, load_sem.at[5]),
+        pltpu.make_async_copy(right_side.at[0], side, load_sem.at[6]),
+        pltpu.make_async_copy(near_values.at[0], values, load_sem.at[7]),
     ]
-    for copy in own + bases + near_loads:
-        copy.start()
-    for copy in own:
-        copy.wait()
+    for copy in bases + near_loads + [own]:
+        copy.start()
 
     pl.semaphore_wait(barrier, panels - 1 + ships - 1)
-    mine = ring.at[pl.ds(panel * blocks, blocks)]
-    spread = to_panels(0, lambda step: mine, lambda step: mine)
+    spread = to_panels(0, lambda step: current.at[0], lambda step: ring.at[panel])
     for copy in spread:
         copy.start()
 
@@ -183,16 +173,21 @@
     for copy in scatter:
         copy.start()
 
-    for copy in near_loads:
+    for copy in near_loads + [own]:
         copy.wait()
     for copy in spread:
         copy.wait_recv()
 
+    def source_block(column):
+        held = ring[column // blocks].reshape(2 * rhs, blocks * block)
+        chosen = held[:, :block]
+        for b in range(1, blocks):
+            chosen = jnp.where(column % blocks == b, held[:, b * block : (b + 1) * block], chosen)
+        return chosen
+
     start_re, start_im = [], []
     for b in range(blocks):
-        picked = jnp.concatenate(
-            [ring[near_columns[0, b, n]].reshape(2 * rhs, block) for n in range(terms)], axis=1
-        )
+        picked = jnp.concatenate([source_block(near_columns[0, b, n]) for n in range(terms)], axis=1)
         weights = jnp.concatenate(
             [values[b, n].reshape(2 * block, block) for n in range(terms)], axis=1
         )
@@ -275,14 +270,14 @@
     anywhere = pl.BlockSpec(memory_space=pl.ANY)
     return pl.pallas_call(
         functools.partial(sweep_kernel, ships, panels),
-        out_shape=jax.ShapeDtypeStruct(right_side.shape, F32),
+        out_shape=pltpu.VMEM(right_side.shape, F32),
         in_specs=[anywhere] * 9,
         out_specs=pl.BlockSpec(memory_space=pltpu.VMEM),
         scratch_shapes=[
             pltpu.SMEM(near_columns.shape, jnp.int32),
             pltpu.SMEM(pair_rank.shape, jnp.int32),
             pltpu.SMEM(plan.shape, jnp.int32),
-            pltpu.VMEM((panels * blocks, 2, rhs, block), BF16),
+            pltpu.VMEM((panels, 2, rhs, blocks * block), BF16),
             pltpu.VMEM(right_side.shape[1:], F32),
             pltpu.VMEM(near_values.shape[1:], BF16),
             pltpu.VMEM(block_inverse.shape[1:], BF16),
@@ -294,7 +289,7 @@
             pltpu.VMEM((rounds, rhs, 2 * rank), BF16),
             pltpu.VMEM((panels - 1, rounds, rhs, 2 * rank), BF16),
             pltpu.VMEM((ships, rounds, rhs, 2 * rank), BF16),
-            pltpu.SemaphoreType.DMA((blocks + 8,)),
+            pltpu.SemaphoreType.DMA((9,)),
             pltpu.SemaphoreType.DMA((4, panels - 1)),
             pltpu.SemaphoreType.DMA((4, panels - 1)),
             pltpu.SemaphoreType.DMA((2, ships - 1)),

time: 22.2 us -> 20.9 us (0.941)
  local copies, waits for them, and re-layouts: 1.47 us -> 0.63 us
  Pallas kernels: 20.6 us -> 20.2 us
    unnamed x1, local copies, waits for them, and re-layouts: 1.47 us -> 0.63 us
    pallas_call x1, Pallas kernels: 20.6 us -> 20.2 us  [few_ships(): pl.pallas_call(functools.partial(sweep_kernel, ships, panels), out_shape=...]
where the time goes in v3:
time: 20.9 us; the launch traced here: 20.8 us
  Pallas kernels  20.2 us (97%)
  local copies, waits for them, and re-layouts  0.63 us (3%)
    pallas_call x1, Pallas kernels, few_ships(): pl.pallas_call(functools.partial(sweep_kernel, ships, panels), out_shape=...  20.2 us
    unnamed x1, local copies, waits for them, and re-layouts  0.63 us

profile of v3, /device:TPU:0, one launch (start us, length us, event | category | flops | bytes accessed | tf_op | source)
XLA Modules:
  0.0 20.8 jit_solution(11370744384962672526)
XLA Ops:
  0.0 20.2 %shard_map.91 = f32[1,2,32,256]{3,2,1,0:T(8,128)S(1)} custom-call(s32[1,2,6]{2,1,0:T(2,128)} %columns_hbm.1, s32[4,4]{1,0:T(4,128)} %rank_hbm.1, s32[3,4]{1,0:T(4,128)} %plan_hbm.1, f32[1,2,32,256]{3,2,1,0:T(8,128)} %right_side.1, bf16[1,2,32,256]{3,2,1,0:T(8,128)(2,1)} %current.1, bf16[1,2,6,2,128,128]{5,4,3,2,1,0:T(8,128)(2,1)} %near_values.1, ...), custom_call_target="tpu_custom_call" | custom-call | tf_op jit(solution)/shard_map/pallas_call | solution.py:271
  20.2 0.6 %copy.11 = f32[1,2,32,256]{3,2,1,0:T(8,128)} copy(f32[1,2,32,256]{3,2,1,0:T(8,128)S(1)} %shard_map.91) | data formatting | bytes 131072
